TPU v7x, 32 devices: a whole 2x2x4 slice. The times are simulated.
32 devices in a mesh: groups: 2 (over y), chan: 4 (over z), tile: 2 (over x), rep: 2 (over core).
Axes of the slice: x: 2, y: 2, z: 4, core: 2. Of those that a mesh axis runs over, the one named last changes fastest.
Arguments:
- generator: float32 [8, 4, 512, 512], P(('groups', 'chan'), ('tile', 'rep')), parts along dimension 0, may hold values from -1.2 to 1.2
- hamiltonian: float32 [8, 4, 512, 512], P(('groups', 'chan'), ('tile', 'rep')), parts along dimension 0, may hold values from -1.2 to 1.2
- pair_weights: float32 [8, 4, 512], P(('groups', 'chan'), ('tile', 'rep')), parts along dimension 0, may hold values from -1 to 1
- cross_weights: float32 [8, 4, 3, 512], P(('groups', 'chan'), ('tile', 'rep')), parts along dimension 0, may hold values from -1 to 1
- recoupling: float32 [8, 16, 16], replicated, may hold values from -1.5 to 1.5
- cross_owner: int32 [8, 4], P('groups', ('tile', 'rep')), parts along dimension 0, may hold values from 0 to 3, as said below
- tile_order: int32 [8, 4, 16], P(('groups', 'chan'), ('tile', 'rep')), parts along dimension 0, may hold values from 0 to 15, each once within a row
- recoupling_index: int32 [8, 4], P('groups', ('tile', 'rep')), parts along dimension 0, may hold values from 0 to 7
Outputs:
- commutator: float32 [8, 4, 512, 512], P(('groups', 'chan'), ('tile', 'rep')), parts along dimension 0
There are 2 independent parts, one for each index of `groups`. A program takes and returns all parts, laid end to end along the dimension named above; an argument that names none is the same for every part. Nothing has to cross between parts.
Inputs may be any that keep to these rules, and one draw needn't show every extreme that they name: `cross_owner`: in every column no owner hosts more than 3 cross-coupled channels, and one owner hosts exactly 3. `tile_order`: each channel's list names every one of its tiles once.
All inputs are finite; a program needn't handle non-finite values.
Results may differ from a plain program's by a relative error of at most 0.0003.
Values sent between devices are 32-bit elements; how exact they have to be, the bound alone decides.
A program may use at most 64 MiB of HBM per device.

v0:
```python
import math

import jax
import jax.numpy as jnp
from jax import lax
from jax.sharding import PartitionSpec as P

TS = 128


highest = lax.Precision.HIGHEST


def to_tiles(matrix, tile_size):
    leading = matrix.shape[:-2]
    blocks = matrix.shape[-1] // tile_size
    shaped = matrix.reshape(leading + (blocks, tile_size, blocks, tile_size))
    shaped = jnp.swapaxes(shaped, -3, -2)
    return shaped.reshape(leading + (blocks * blocks, tile_size, tile_size))


def from_tiles(pieces, tile_size):
    leading = pieces.shape[:-3]
    blocks = math.isqrt(pieces.shape[-3])
    shaped = pieces.reshape(leading + (blocks, blocks, tile_size, tile_size))
    shaped = jnp.swapaxes(shaped, -3, -2)
    return shaped.reshape(leading + (blocks * tile_size, blocks * tile_size))


def bracket(left_matrix, right_matrix, weights):
    scaled = weights[..., None, :]
    left_term = jnp.matmul(left_matrix * scaled, right_matrix, precision=highest)
    right_term = jnp.matmul(right_matrix * scaled, left_matrix, precision=highest)
    return left_term - right_term


def cross_term(generator_cross, hamilton_cross, mixers, weights):
    generator_mixed = jnp.einsum("csji,csixy->csjxy", mixers, generator_cross, precision=highest)
    hamilton_mixed = jnp.einsum("csji,csixy->csjxy", mixers, hamilton_cross, precision=highest)
    product = bracket(from_tiles(generator_mixed, TS), from_tiles(hamilton_mixed, TS), weights)
    return jnp.einsum("csji,csjxy->csixy", mixers, to_tiles(product, TS), precision=highest)


def body(
    generator,
    hamiltonian,
    pair_weights,
    cross_weights,
    recoupling,
    cross_owner,
    tile_order,
    recoupling_index,
):
    channels = cross_owner.shape[0]
    column_count = generator.shape[1]
    tile_count = tile_order.shape[-1]
    spread = tile_count // channels
    capacity = cross_weights.shape[2]
    my_index = lax.axis_index("chan")
    chan_range = jnp.arange(channels, dtype=jnp.int32)
    tile_range = jnp.arange(tile_count, dtype=jnp.int32)
    spread_range = jnp.arange(spread, dtype=jnp.int32)
    column_range = jnp.arange(column_count, dtype=jnp.int32)
    slot_range = jnp.arange(capacity, dtype=jnp.int32)
    generator_tiles = to_tiles(generator[0], TS)
    hamilton_tiles = to_tiles(hamiltonian[0], TS)
    orders = tile_order[0]
    owners = jnp.transpose(cross_owner)
    mixer_index = jnp.transpose(recoupling_index)
    same_owner = owners[:, :, None] == owners[:, None, :]
    earlier = chan_range[None, :] < chan_range[:, None]
    slot_of = jnp.sum((same_owner & earlier[None]).astype(jnp.int32), axis=2)
    inverse = jnp.sum(
        jnp.where(orders[:, :, None] == tile_range[None, None, :], tile_range[None, :, None], 0),
        axis=1,
    )
    target = inverse // spread
    target_rank = inverse % spread
    column_index = column_range[:, None, None, None]
    hosting = (owners[:, :, None, None] == chan_range[None, None, :, None]) & (
        slot_of[:, :, None, None] == slot_range[None, None, None, :]
    )
    hosted = jnp.sum(jnp.where(hosting, chan_range[None, :, None, None], 0), axis=1)
    filled = jnp.any(hosting, axis=1)
    ordinal = hosted[:, :, :, None] * spread + spread_range[None, None, None, :]
    chosen = jnp.take_along_axis(orders, ordinal.reshape(column_count, -1), axis=1).reshape(
        ordinal.shape
    )
    chosen = jnp.transpose(chosen, (0, 2, 3, 1))
    keeping = jnp.transpose(filled, (0, 2, 1))[:, :, None, :, None, None]
    generator_send = jnp.where(keeping, generator_tiles[column_index, chosen], 0.0)
    hamilton_send = jnp.where(keeping, hamilton_tiles[column_index, chosen], 0.0)
    generator_got, hamilton_got = (
        lax.all_to_all(generator_send, "chan", split_axis=3, concat_axis=3, tiled=True),
        lax.all_to_all(hamilton_send, "chan", split_axis=3, concat_axis=3, tiled=True),
    )
    hosted_here = jnp.take(hosted, my_index, axis=1)
    mixers = recoupling[jnp.take_along_axis(mixer_index, hosted_here, axis=1)]
    weights_cross = cross_weights[0]
    shape_back = (column_count, capacity, tile_count, TS, TS)
    returned = cross_term(
        generator_got.reshape(shape_back), hamilton_got.reshape(shape_back), mixers, weights_cross
    )
    returned_home = lax.all_to_all(
        returned.reshape(column_count, capacity, spread, channels, TS, TS),
        "chan",
        split_axis=3,
        concat_axis=3,
        tiled=True,
    )
    from_slot = jnp.take_along_axis(slot_of, target, axis=1)
    from_device = jnp.take_along_axis(owners, target, axis=1)
    back_tiles = returned_home[column_range[:, None], from_slot, target_rank, from_device]
    direct = bracket(generator[0], hamiltonian[0], pair_weights[0])
    summed = direct + from_tiles(back_tiles, TS)
    return (0.5 * (summed + jnp.swapaxes(summed, -1, -2)))[None]


def solution(mesh):
    placed = (
        P(("groups", "chan"), ("tile", "rep"), None, None),
        P(("groups", "chan"), ("tile", "rep"), None, None),
        P(("groups", "chan"), ("tile", "rep"), None),
        P(("groups", "chan"), ("tile", "rep"), None, None),
        P(),
        P("groups", ("tile", "rep")),
        P(("groups", "chan"), ("tile", "rep"), None),
        P("groups", ("tile", "rep")),
    )
    return jax.shard_map(
        body,
        mesh=mesh,
        in_specs=placed,
        out_specs=P(("groups", "chan"), ("tile", "rep"), None, None),
        check_vma=False,
    )
```

profile of v0, /device:TPU:12, one launch (start us, length us, event | category | flops | bytes accessed | tf_op | source)
XLA Modules:
  0.0 288.8 jit_solution(5570581685007703052)
XLA Ops:
  0.0 0.0 copy-start
  0.0 0.9 convert_reduce_fusion
  1.0 0.7 iota_compare_fusion.3
  1.7 0.1 fusion.31
  1.8 0.1 and_reduce_fusion
  1.9 0.1 copy.83
  2.0 0.1 iota_add_fusion
  2.0 0.1 add.231
  2.2 1.4 gather_fusion.2
  3.6 0.1 gather.36
  3.7 0.1 compare_select_fusion
  3.8 0.1 copy.85
  3.9 0.1 reshape.859
  4.0 1.6 reshape_squeeze.6
  5.6 0.1 copy.82
  5.7 0.0 copy-done.6
  5.7 0.4 reshape_squeeze.7
  6.1 0.1 copy.90
  6.2 2.5 gather_fusion.3
  8.7 2.5 gather_fusion.4
  11.2 0.1 copy.80
  11.3 0.1 copy.81
  11.4 5.4 %broadcast_select_fusion = (f32[1,3,4,4,128,128]{5,4,3,2,1,0:T(8,128)}, f32[1,3,4,4,128,128]{5,4,3,2,1,0:T(8,128)S(1)}) fusion(f32[1,3,4,4,128,128]{5,4,3,2,1,0:T(8,128)} %bitcast.161, pred[3,4]{1,0:T(4,128)(4,1)S(1)} %bitcast.171, f32[1,3,4,4,128,128]{5,4,3,2,1,0:T(8,128)} %bitcast.160), kind=kLoop, calls=%fused_computation.15 | loop fusion | flops 1572864 | bytes 12582924 | tf_op jit(solution)/shard_map/jit(_where)/select_n | solution.py:92
  16.9 1.9 copy.87
  18.8 5.3 %all-to-all-start = ((f32[1,3,4,4,128,128]{5,4,2,1,0,3:T(8,128)}), f32[1,3,4,4,128,128]{5,4,2,1,0,3:T(8,128)S(1)}, u32[]{:S(2)}, u32[]{:S(2)}) async-start(f32[1,3,4,4,128,128]{5,4,2,1,0,3:T(8,128)} %copy.87), calls=%async_computation | async-start | bytes 6291456 | tf_op jit(solution)/shard_map/all_to_all | solution.py:94
  24.1 3.9 %copy.91 = f32[1,3,4,4,128,128]{5,4,2,1,0,3:T(8,128)} copy(f32[1,3,4,4,128,128]{5,4,3,2,1,0:T(8,128)} %get-tuple-element.19) | data formatting | bytes 6291456 | tf_op jit(solution)/shard_map/jit(_where)/select_n | solution.py:92
  28.0 63.5 %all-to-all-done = f32[1,3,4,4,128,128]{5,4,2,1,0,3:T(8,128)S(1)} async-done(((f32[1,3,4,4,128,128]{5,4,2,1,0,3:T(8,128)}), f32[1,3,4,4,128,128]{5,4,2,1,0,3:T(8,128)S(1)}, u32[]{:S(2)}, u32[]{:S(2)}) %all-to-all-start) | async-done | bytes 3145760 | tf_op jit(solution)/shard_map/all_to_all | solution.py:94
  91.5 7.9 %all-to-all-start.1 = ((f32[1,3,4,4,128,128]{5,4,2,1,0,3:T(8,128)}), f32[1,3,4,4,128,128]{5,4,2,1,0,3:T(8,128)}, u32[]{:S(2)}, u32[]{:S(2)}) async-start(f32[1,3,4,4,128,128]{5,4,2,1,0,3:T(8,128)} %copy.91), calls=%async_computation.1 | async-start | bytes 6291456 | tf_op jit(solution)/shard_map/all_to_all | solution.py:95
  99.3 0.0 copy-done.10
  99.3 0.2 select_reduce_fusion.1
  99.5 0.0 copy-done.2
  99.6 0.6 gather_fusion
  100.2 0.0 copy-done
  100.2 0.6 gather_fusion.1
  100.8 2.0 copy.88
  102.8 2.9 %fusion.24 = f32[3,16,128,128]{3,1,2,0:T(8,128)S(1)} fusion(f32[3,16,128,128]{3,1,2,0:T(8,128)S(1)} %bitcast.155, f32[3,16,16]{2,1,0:T(8,128)S(1)} %gather_fusion.1), kind=kOutput, calls=%fused_computation.34 | convolution fusion | flops 150994944 | bytes 6294528 | tf_op jit(solution)/shard_map/csji,csixy->csjxy/dot_general | solution.py:38
  105.7 2.4 copy.89
  108.2 3.3 %reshape.759 = f32[3,512,512]{2,1,0:T(8,128)S(1)} reshape(f32[1,3,4,128,4,128]{5,4,3,2,1,0:T(4,128)} %copy.89) | data formatting | bytes 6291456 | tf_op jit(solution)/shard_map/reshape | solution.py:27
  111.5 54.8 %all-to-all-done.1 = f32[1,3,4,4,128,128]{5,4,2,1,0,3:T(8,128)} async-done(((f32[1,3,4,4,128,128]{5,4,2,1,0,3:T(8,128)}), f32[1,3,4,4,128,128]{5,4,2,1,0,3:T(8,128)}, u32[]{:S(2)}, u32[]{:S(2)}) %all-to-all-start.1) | async-done | bytes 3145760 | tf_op jit(solution)/shard_map/all_to_all | solution.py:95
  166.2 3.9 %copy.92 = f32[1,3,4,4,128,128]{5,3,2,4,1,0:T(4,128)S(1)} copy(f32[1,3,4,4,128,128]{5,4,2,1,0,3:T(8,128)} %all-to-all-done.1) | data formatting | bytes 6291456 | tf_op jit(solution)/shard_map/all_to_all | solution.py:95
  170.2 2.9 %fusion.22 = f32[3,16,128,128]{3,1,2,0:T(8,128)S(1)} fusion(f32[3,16,128,128]{3,1,2,0:T(8,128)S(1)} %bitcast.157, f32[3,16,16]{2,1,0:T(8,128)S(1)} %gather_fusion.1), kind=kOutput, calls=%fused_computation.32 | convolution fusion | flops 150994944 | bytes 6294528 | tf_op jit(solution)/shard_map/csji,csixy->csjxy/dot_general | solution.py:39
  173.1 2.4 copy.93
  175.5 5.1 %squeeze_reshape.4 = f32[3,512,512]{2,1,0:T(8,128)} reshape(f32[1,3,4,128,4,128]{5,4,3,2,1,0:T(4,128)} %copy.93) | data formatting | bytes 6291456 | tf_op jit(solution)/shard_map/squeeze;reshape | solution.py:32
  180.5 7.6 %fusion = f32[3,512,512]{2,1,0:T(8,128)S(1)} fusion(f32[3,512,512]{2,1,0:T(8,128)S(1)} %reshape.759, f32[3,512,512]{2,1,0:T(8,128)} %squeeze_reshape.4, f32[3,512]{1,0:T(4,128)S(1)} %bitcast.166), kind=kOutput, calls=%fused_computation.8 | convolution fusion | flops 4832624640 | bytes 9443328 | tf_op jit(solution)/shard_map/dot_general | solution.py:33
  188.1 0.0 copy-done.5
  188.1 7.1 %fusion.4 = f32[3,512,512]{2,1,0:T(8,128)} fusion(f32[3,512,512]{2,1,0:T(8,128)S(1)} %fusion, f32[3,512,512]{2,1,0:T(8,128)S(1)} %copy-done.5, f32[3,512,512]{2,1,0:T(8,128)S(1)} %reshape.759, f32[3,512]{1,0:T(4,128)S(1)} %bitcast.167), kind=kOutput, calls=%fused_computation.12 | convolution fusion | flops 4833411072 | bytes 12589056 | tf_op jit(solution)/shard_map/dot_general | solution.py:32
  195.3 3.4 %reshape.763 = f32[1,3,4,128,4,128]{5,4,3,2,1,0:T(4,128)S(1)} reshape(f32[3,512,512]{2,1,0:T(8,128)} %fusion.4) | data formatting | bytes 6291456 | tf_op jit(solution)/shard_map/reshape | solution.py:17
  198.7 0.5 copy.94
  199.2 3.0 %fusion.26 = f32[3,16,128,128]{3,1,2,0:T(8,128)S(1)} fusion(f32[3,16,128,128]{3,1,2,0:T(8,128)S(1)} %bitcast.153, f32[3,16,16]{2,1,0:T(8,128)S(1)} %gather_fusion.1), kind=kOutput, calls=%fused_computation.36 | convolution fusion | flops 150994944 | bytes 6294528 | tf_op jit(solution)/shard_map/csji,csjxy->csixy/dot_general | solution.py:41
  202.2 2.6 copy.96
  204.8 7.2 %all-to-all-start.2 = ((f32[1,3,4,4,128,128]{5,4,2,1,0,3:T(8,128)}), f32[1,3,4,4,128,128]{5,4,2,1,0,3:T(8,128)S(1)}, u32[]{:S(2)}, u32[]{:S(2)}) async-start(f32[1,3,4,4,128,128]{5,4,2,1,0,3:T(8,128)} %copy.96), calls=%async_computation.2 | async-start | bytes 6291456 | tf_op jit(solution)/shard_map/all_to_all | solution.py:104
  212.0 0.0 copy-done.3
  212.0 0.1 select_reduce_fusion
  212.1 0.7 gather_fusion.6
  212.8 0.7 gather_fusion.7
  213.5 4.4 %fusion.15 = f32[512,512]{1,0:T(8,128)} fusion(f32[1,1,512,512]{3,2,1,0:T(8,128)} %param.11, f32[1,1,512,512]{3,2,1,0:T(8,128)} %param.10, f32[512]{0:T(512)S(1)} %bitcast.169), kind=kOutput, calls=%fused_computation.25 | convolution fusion | flops 1610874880 | bytes 3147776 | tf_op jit(solution)/shard_map/dot_general | solution.py:32
  217.9 61.0 %all-to-all-done.2 = f32[1,3,4,4,128,128]{5,4,2,1,0,3:T(8,128)S(1)} async-done(((f32[1,3,4,4,128,128]{5,4,2,1,0,3:T(8,128)}), f32[1,3,4,4,128,128]{5,4,2,1,0,3:T(8,128)S(1)}, u32[]{:S(2)}, u32[]{:S(2)}) %all-to-all-start.2) | async-done | bytes 3145760 | tf_op jit(solution)/shard_map/all_to_all | solution.py:104
  278.9 1.8 copy.97
  280.7 2.7 gather_fusion.5
  283.4 0.7 copy.98
  284.1 0.0 copy-start.1
  284.1 3.2 %fusion.10 = f32[1,512,512]{2,1,0:T(8,128)S(1)} fusion(f32[512,512]{1,0:T(8,128)} %fusion.15, f32[64,8,4,128]{3,2,1,0:T(4,128)S(1)} %bitcast.162, f32[1,1,512,512]{3,2,1,0:T(8,128)S(1)} %copy-done.8, f32[1,1,512,512]{3,2,1,0:T(8,128)S(1)} %copy-done.7, f32[512]{0:T(512)S(1)} %bitcast.170), kind=kOutput, calls=%fused_computation.19 | convolution fusion | flops 1611399168 | bytes 5244928 | tf_op jit(solution)/shard_map/dot_general | solution.py:33
  287.3 0.3 copy.99
  287.6 1.2 fusion.12
  (32 shorter events, 0.2 us)
Async XLA Ops:
  0.0 100.2 %copy-start = (f32[8,16,16]{2,1,0:T(8,128)S(1)}, f32[8,16,16]{2,1,0:T(8,128)}, u32[]{:S(2)}) copy-start(f32[8,16,16]{2,1,0:T(8,128)} %param.14) | copy-start | bytes 24580
  0.0 5.7 %copy-start.6 = (f32[1,1,512,512]{3,2,1,0:T(8,128)S(1)}, f32[1,1,512,512]{3,2,1,0:T(8,128)}, u32[]{:S(2)}) copy-start(f32[1,1,512,512]{3,2,1,0:T(8,128)} %param.11) | copy-start | bytes 3145732
  18.8 72.7 %all-to-all-start = ((f32[1,3,4,4,128,128]{5,4,2,1,0,3:T(8,128)}), f32[1,3,4,4,128,128]{5,4,2,1,0,3:T(8,128)S(1)}, u32[]{:S(2)}, u32[]{:S(2)}) async-start(f32[1,3,4,4,128,128]{5,4,2,1,0,3:T(8,128)} %copy.87), calls=%async_computation | async-start | bytes 6291456 | tf_op jit(solution)/shard_map/all_to_all | solution.py:94
  28.0 71.4 %copy-start.10 = (f32[1,1,3,512]{3,1,2,0:T(1,128)S(1)}, f32[1,1,3,512]{3,1,2,0:T(1,128)}, u32[]{:S(2)}) copy-start(f32[1,1,3,512]{3,1,2,0:T(1,128)} %param.13) | copy-start | bytes 18436
  28.0 71.6 %copy-start.2 = (s32[4,1]{0,1:T(1,128)S(1)}, s32[4,1]{0,1:T(1,128)}, u32[]{:S(2)}) copy-start(s32[4,1]{0,1:T(1,128)} %param.17) | copy-start | bytes 52
  91.5 74.8 %all-to-all-start.1 = ((f32[1,3,4,4,128,128]{5,4,2,1,0,3:T(8,128)}), f32[1,3,4,4,128,128]{5,4,2,1,0,3:T(8,128)}, u32[]{:S(2)}, u32[]{:S(2)}) async-start(f32[1,3,4,4,128,128]{5,4,2,1,0,3:T(8,128)} %copy.91), calls=%async_computation.1 | async-start | bytes 6291456 | tf_op jit(solution)/shard_map/all_to_all | solution.py:95
  180.5 7.6 %copy-start.5 = (f32[3,512,512]{2,1,0:T(8,128)S(1)}, f32[3,512,512]{2,1,0:T(8,128)}, u32[]{:S(2)}) copy-start(f32[3,512,512]{2,1,0:T(8,128)} %squeeze_reshape.4) | copy-start | bytes 9437188
  204.8 7.2 %copy-start.3 = (s32[1,1,16]{2,1,0:T(1,128)S(1)}, s32[1,1,16]{2,1,0:T(1,128)}, u32[]{:S(2)}) copy-start(s32[1,1,16]{2,1,0:T(1,128)} %param.16) | copy-start | bytes 196
  204.8 8.0 %copy-start.4 = (s32[4,1]{0,1:T(1,128)S(1)}, s32[4,1]{0,1:T(1,128)}, u32[]{:S(2)}) copy-start(s32[4,1]{0,1:T(1,128)} %param.15) | copy-start | bytes 52
  204.8 8.7 %copy-start.9 = (f32[1,1,512]{2,1,0:T(1,128)S(1)}, f32[1,1,512]{2,1,0:T(1,128)}, u32[]{:S(2)}) copy-start(f32[1,1,512]{2,1,0:T(1,128)} %param.12) | copy-start | bytes 6148
  204.8 74.1 %all-to-all-start.2 = ((f32[1,3,4,4,128,128]{5,4,2,1,0,3:T(8,128)}), f32[1,3,4,4,128,128]{5,4,2,1,0,3:T(8,128)S(1)}, u32[]{:S(2)}, u32[]{:S(2)}) async-start(f32[1,3,4,4,128,128]{5,4,2,1,0,3:T(8,128)} %copy.96), calls=%async_computation.2 | async-start | bytes 6291456 | tf_op jit(solution)/shard_map/all_to_all | solution.py:104
  280.7 3.4 %copy-start.7 = (f32[1,1,512,512]{3,2,1,0:T(8,128)S(1)}, f32[1,1,512,512]{3,2,1,0:T(8,128)}, u32[]{:S(2)}) copy-start(f32[1,1,512,512]{3,2,1,0:T(8,128)} %param.11) | copy-start | bytes 3145732
  280.7 3.4 %copy-start.8 = (f32[1,1,512,512]{3,2,1,0:T(8,128)S(1)}, f32[1,1,512,512]{3,2,1,0:T(8,128)}, u32[]{:S(2)}) copy-start(f32[1,1,512,512]{3,2,1,0:T(8,128)} %param.10) | copy-start | bytes 3145732
  284.1 4.8 %copy-start.1 = (f32[8,16,16]{2,1,0:T(8,128)S(1)}, f32[8,16,16]{2,1,0:T(8,128)}, u32[]{:S(2)}) copy-start(f32[8,16,16]{2,1,0:T(8,128)} %param.14) | copy-start | bytes 24580
where the time goes:
time: 294 us; the launch traced here: 289 us
  waiting for transfers between devices  179 us (61%)
  local copies, waits for them, and re-layouts  48.8 us (17%)
  matrix products  31.1 us (11%)
  starting transfers between devices  20.4 us (7%)
  other arithmetic  9.05 us (3%)
    all_to_all x1, waiting for transfers between devices, body(): lax.all_to_all(generator_send, 'chan', split_axis=3, concat_axis=3, tiled...  63.5 us
    all_to_all x1, waiting for transfers between devices, body(): lax.all_to_all(returned.reshape(column_count, capacity, spread, channels,...  61 us
    all_to_all x1, waiting for transfers between devices, body(): lax.all_to_all(hamilton_send, 'chan', split_axis=3, concat_axis=3, tiled=...  54.8 us
    dot_general x2, matrix products, bracket(): jnp.matmul(left_matrix * scaled, right_matrix, precision=highest)  11.5 us
    dot_general x2, matrix products, bracket(): jnp.matmul(right_matrix * scaled, left_matrix, precision=highest)  10.8 us
    all_to_all x1, starting transfers between devices, body(): lax.all_to_all(hamilton_send, 'chan', split_axis=3, concat_axis=3, tiled=...  7.87 us
    all_to_all x1, starting transfers between devices, body(): lax.all_to_all(returned.reshape(column_count, capacity, spread, channels,...  7.18 us
  transfers between devices with their start and end apart: 3, of which 3 were waited for; matrix products, arithmetic and copies ran while one was open for 8% of the time, Pallas kernels for 0%

commit v1 on v0

v1 whole, which is shorter than its diff:
```python
import functools

import jax
import jax.numpy as jnp
from jax import lax
from jax.experimental import pallas as pl
from jax.experimental.pallas import tpu as pltpu
from jax.sharding import PartitionSpec as P

TS = 128
CHUNK = 32
SUB = 16
WIDE = 256
MESH = pl.DeviceIdType.MESH


def split(x):
    high = x.astype(jnp.bfloat16)
    return high, (x - high.astype(jnp.float32)).astype(jnp.bfloat16)


def store_factor(left, right, s, rows, cols, x, weights):
    high, low = split(x * weights)
    left[2 * s, rows, cols] = high
    left[2 * s + 1, rows, cols] = low
    high, low = split(x)
    right[2 * (1 - s), rows, cols] = high
    right[2 * (1 - s) + 1, rows, cols] = low


def bracket(left, right, out):
    order = out.shape[0]

    def part(c, carry):
        cols = pl.ds(pl.multiple_of(c * WIDE, WIDE), WIDE)
        total = None
        for at_left, at_right in ((0, 0), (1, 0), (0, 1), (2, 2), (3, 2), (2, 3)):
            term = jnp.dot(
                left[at_left], right[at_right, :, cols], preferred_element_type=jnp.float32
            )
            total = term if total is None else total + term
        out[:, cols] = total
        return carry

    lax.fori_loop(0, order // WIDE, part, 0)


def kernel(
    n,
    generator,
    hamiltonian,
    pair_weights,
    cross_weights,
    recoupling,
    cross_owner,
    tile_order,
    recoupling_index,
    out,
    generator_tiles,
    hamilton_tiles,
    send,
    recv,
    weights_send,
    weights_recv,
    left,
    right,
    product,
    direct,
    back_send,
    back,
    back_turned,
    inverse,
    send_sem,
    recv_sem,
    weights_send_sem,
    weights_recv_sem,
    back_send_sem,
    back_recv_sem,
):
    me = lax.axis_index("chan")
    order = generator.shape[-1]
    blocks = order // TS
    tiles = tile_order.shape[-1]
    spread = tiles // n
    chunks = TS // CHUNK
    hosted = cross_weights.shape[2]

    def partner(d):
        p, bit = me, 1
        while bit <= d:
            if d & bit:
                p = p + bit * (1 - 2 * lax.rem(lax.div(me, bit), 2))
            bit *= 2
        return p

    distances = sorted(range(1, n), key=lambda d: -d.bit_length())
    partners = {d: partner(d) for d in range(1, n)}

    barrier = pltpu.get_barrier_semaphore()
    for d in distances:
        pl.semaphore_signal(barrier, inc=1, device_id={"chan": partners[d]}, device_id_type=MESH)

    for slot in range(hosted):
        weights_send[slot] = cross_weights[0, 0, slot : slot + 1, :]
    weights_recv[me] = weights_send[...]
    for q in range(tiles):
        here, there = pl.ds((q // blocks) * TS, TS), pl.ds((q % blocks) * TS, TS)
        generator_tiles[q] = generator[0, 0, here, there]
        hamilton_tiles[q] = hamiltonian[0, 0, here, there]

    def pack(ch, target, slot):
        for r in range(spread):
            q = tile_order[0, 0, target * spread + r]
            rows = pl.ds(pl.multiple_of(ch * CHUNK, CHUNK), CHUNK)
            slot[0, r] = generator_tiles[q, rows, :]
            slot[1, r] = hamilton_tiles[q, rows, :]

    def weights_copy(d, at):
        return pltpu.make_async_remote_copy(
            src_ref=weights_send,
            dst_ref=weights_recv.at[at],
            send_sem=weights_send_sem.at[d],
            recv_sem=weights_recv_sem.at[d],
            device_id={"chan": partners[d]},
            device_id_type=MESH,
        )

    def tiles_copy(ch, d, at):
        return pltpu.make_async_remote_copy(
            src_ref=send.at[ch, d],
            dst_ref=recv.at[ch, at],
            send_sem=send_sem.at[ch, d],
            recv_sem=recv_sem.at[ch, d],
            device_id={"chan": partners[d]},
            device_id_type=MESH,
        )

    def back_copy(d, at):
        return pltpu.make_async_remote_copy(
            src_ref=back_send.at[d],
            dst_ref=back.at[at],
            send_sem=back_send_sem.at[d],
            recv_sem=back_recv_sem.at[d],
            device_id={"chan": partners[d]},
            device_id_type=MESH,
        )

    def pack_partners(ch, carry):
        for d in distances:
            pack(ch, partners[d], send.at[ch, d])
        return carry

    def start_chunk(ch, carry):
        for d in distances:
            tiles_copy(ch, d, me).start()
        return carry

    pack_partners(0, 0)
    pl.semaphore_wait(barrier, n - 1)
    for d in distances:
        weights_copy(d, me).start()
    start_chunk(0, 0)

    def pack_and_start(ch, carry):
        pack_partners(ch, 0)
        return start_chunk(ch, carry)

    lax.fori_loop(1, chunks, pack_and_start, 0)

    def pack_own(ch, carry):
        pack(ch, me, recv.at[ch, me])
        return carry

    lax.fori_loop(0, chunks, pack_own, 0)

    pair_row = pair_weights[0]

    def split_direct(step, carry):
        rows = pl.ds(pl.multiple_of(step * SUB, SUB), SUB)
        every = slice(None)
        store_factor(left, right, 0, rows, every, generator[0, 0, rows, :], pair_row)
        store_factor(left, right, 1, rows, every, hamiltonian[0, 0, rows, :], -pair_row)
        return carry

    lax.fori_loop(0, order // SUB, split_direct, 0)
    bracket(left, right, product)
    for a in range(blocks):
        for b in range(blocks):
            here, there = pl.ds(a * TS, TS), pl.ds(b * TS, TS)
            direct[here, there] = 0.5 * (product[here, there] + product[there, here].T)

    def invert(q, carry):
        at = jnp.int32(0)
        for t in range(tiles):
            at = jnp.maximum(at, jnp.where(tile_order[0, 0, t] == q, t, 0))
        inverse[q] = at
        return carry

    lax.fori_loop(0, tiles, invert, 0)

    owner = cross_owner[me, 0]
    slot_at = jnp.int32(0)
    for g in range(n):
        slot_at = slot_at + jnp.where(
            jnp.logical_and(g < me, cross_owner[g, 0] == owner), 1, 0
        )
    slot_at = jnp.minimum(slot_at, hosted - 1)
    for d in distances:
        weights_copy(d, partners[d]).wait_recv()
    cross_row = weights_recv[owner, slot_at]
    matrix = recoupling_index[me, 0]

    def mix_chunk(ch, carry):
        for d in distances:
            tiles_copy(ch, d, partners[d]).wait_recv()

        def mix(step, inner):
            s, part = lax.div(step, CHUNK // SUB), lax.rem(step, CHUNK // SUB)
            rows = pl.ds(pl.multiple_of(part * SUB, SUB), SUB)
            signed = cross_row * (1 - 2 * s).astype(jnp.float32)
            taken = [recv[ch, i % n, s, i // n, rows, :] for i in range(tiles)]
            for j in range(tiles):
                total = taken[0] * recoupling[matrix, j, 0]
                for i in range(1, tiles):
                    total = total + taken[i] * recoupling[matrix, j, i]
                start = (j // blocks) * TS + ch * CHUNK + part * SUB
                to_rows = pl.ds(pl.multiple_of(start, SUB), SUB)
                cols = slice((j % blocks) * TS, (j % blocks + 1) * TS)
                store_factor(left, right, s, to_rows, cols, total, signed[:, cols])
            return inner

        return lax.fori_loop(0, 2 * (CHUNK // SUB), mix, carry)

    lax.fori_loop(0, chunks, mix_chunk, 0)
    bracket(left, right, product)

    def mix_back(home, slot):
        def part(c, carry):
            rows = pl.ds(pl.multiple_of(c * CHUNK, CHUNK), CHUNK)
            totals = [None] * spread
            for j in range(tiles):
                start = (j // blocks) * TS + c * CHUNK
                from_rows = pl.ds(pl.multiple_of(start, CHUNK), CHUNK)
                piece = product[from_rows, (j % blocks) * TS : (j % blocks + 1) * TS]
                for r in range(spread):
                    term = piece * recoupling[matrix, j, r * n + home]
                    totals[r] = term if j == 0 else totals[r] + term
            for r in range(spread):
                slot[r, rows, :] = totals[r]
            return carry

        lax.fori_loop(0, chunks, part, 0)

    for d in distances:
        mix_back(partners[d], back_send.at[d])
        back_copy(d, me).start()
    mix_back(me, back.at[me])

    def turn(source):
        for r in range(spread):
            back_turned[source, r] = back[source, r].T

    turn(me)
    for d in reversed(distances):
        back_copy(d, partners[d]).wait_recv()
        turn(partners[d])

    for q in range(tiles):
        a, b = q // blocks, q % blocks
        at, turned_at = inverse[q], inverse[b * blocks + a]
        came = back[lax.div(at, spread), lax.rem(at, spread)]
        turned = back_turned[lax.div(turned_at, spread), lax.rem(turned_at, spread)]
        here, there = pl.ds(a * TS, TS), pl.ds(b * TS, TS)
        out[0, 0, here, there] = direct[here, there] + 0.5 * (came + turned)

    for d in distances:
        weights_copy(d, me).wait_send()
        back_copy(d, me).wait_send()

    def finish(ch, carry):
        for d in distances:
            tiles_copy(ch, d, me).wait_send()
        return carry

    lax.fori_loop(0, chunks, finish, 0)


def solution(mesh):
    n = mesh.shape["chan"]
    placed = (
        P(("groups", "chan"), ("tile", "rep"), None, None),
        P(("groups", "chan"), ("tile", "rep"), None, None),
        P(("groups", "chan"), ("tile", "rep"), None),
        P(("groups", "chan"), ("tile", "rep"), None, None),
        P(),
        P("groups", ("tile", "rep")),
        P(("groups", "chan"), ("tile", "rep"), None),
        P("groups", ("tile", "rep")),
    )

    def body(
        generator,
        hamiltonian,
        pair_weights,
        cross_weights,
        recoupling,
        cross_owner,
        tile_order,
        recoupling_index,
    ):
        order = generator.shape[-1]
        tiles = tile_order.shape[-1]
        spread = tiles // n
        chunks = TS // CHUNK
        hosted = cross_weights.shape[2]
        f32, bf16 = jnp.float32, jnp.bfloat16
        vmem = pl.BlockSpec(memory_space=pltpu.VMEM)
        smem = pl.BlockSpec(memory_space=pltpu.SMEM)
        return pl.pallas_call(
            functools.partial(kernel, n),
            out_shape=jax.ShapeDtypeStruct(generator.shape, f32),
            in_specs=[vmem] * 4 + [smem] * 4,
            out_specs=vmem,
            scratch_shapes=[
                pltpu.VMEM((tiles, TS, TS), f32),
                pltpu.VMEM((tiles, TS, TS), f32),
                pltpu.VMEM((chunks, n, 2, spread, CHUNK, TS), f32),
                pltpu.VMEM((chunks, n, 2, spread, CHUNK, TS), f32),
                pltpu.VMEM((hosted, 1, order), f32),
                pltpu.VMEM((n, hosted, 1, order), f32),
                pltpu.VMEM((4, order, order), bf16),
                pltpu.VMEM((4, order, order), bf16),
                pltpu.VMEM((order, order), f32),
                pltpu.VMEM((order, order), f32),
                pltpu.VMEM((n, spread, TS, TS), f32),
                pltpu.VMEM((n, spread, TS, TS), f32),
                pltpu.VMEM((n, spread, TS, TS), f32),
                pltpu.SMEM((tiles,), jnp.int32),
                pltpu.SemaphoreType.DMA((chunks, n)),
                pltpu.SemaphoreType.DMA((chunks, n)),
                pltpu.SemaphoreType.DMA((n,)),
                pltpu.SemaphoreType.DMA((n,)),
                pltpu.SemaphoreType.DMA((n,)),
                pltpu.SemaphoreType.DMA((n,)),
            ],
            compiler_params=pltpu.CompilerParams(
                collective_id=0, has_side_effects=True, vmem_limit_bytes=48 * 1024 * 1024
            ),
        )(
            generator,
            hamiltonian,
            pair_weights,
            cross_weights,
            recoupling,
            cross_owner,
            tile_order,
            recoupling_index,
        )

    return jax.shard_map(
        body,
        mesh=mesh,
        in_specs=placed,
        out_specs=P(("groups", "chan"), ("tile", "rep"), None, None),
        check_vma=False,
    )
```

time: 294 us -> 83.3 us (0.28); the launches traced: 289 us -> 82.9 us
  waiting for transfers between devices: 179 us -> 0 us
  Pallas kernels: 0 us -> 77 us
  local copies, waits for them, and re-layouts: 48.8 us -> 5.83 us
  matrix products: 31.1 us -> 0 us
  starting transfers between devices: 20.4 us -> 0 us
  other arithmetic: 9.05 us -> 0 us
    all_to_all x3 -> x0, waiting for transfers between devices: 179 us -> none  [the longest x1 63.5 us: body(): lax.all_to_all(generator_send, 'chan', split_axis=3, concat_axis=3, tiled...]
    pallas_call x0 -> x1, Pallas kernels: none -> 77 us  [body(): pl.pallas_call(functools.partial(kernel, n), out_shape=jax.ShapeDtypeStru...]
    dot_general x7 -> x0, matrix products: 31.1 us -> none  [the longest x2 11.5 us: bracket(): jnp.matmul(left_matrix * scaled, right_matrix, precision=highest)]
    all_to_all x3 -> x0, starting transfers between devices: 20.4 us -> none  [the longest x1 7.87 us: body(): lax.all_to_all(hamilton_send, 'chan', split_axis=3, concat_axis=3, tiled=...]
    gather x9 -> x0, local copies, waits for them, and re-layouts: 11.7 us -> none  [the longest x1 2.65 us: body(): returned_home[column_range[:, None], from_slot, target_rank, from_device]]
    reshape x3 -> x0, local copies, waits for them, and re-layouts: 9.32 us -> none  [the longest x1 3.4 us: to_tiles(): shaped = matrix.reshape(leading + (blocks, tile_size, blocks, tile_size))]
    all_to_all x3 -> x0, local copies, waits for them, and re-layouts: 7.78 us -> none  [the longest x1 3.91 us: body(): lax.all_to_all(hamilton_send, 'chan', split_axis=3, concat_axis=3, tiled=...]
    another operation x4 -> x0, local copies, waits for them, and re-layouts: 6.99 us -> none  [the longest x1 5.06 us: bracket(): jnp.matmul(left_matrix * scaled, right_matrix, precision=highest)]
  transfers between devices with their start and end apart: 3 -> 0, of which waited for: 3 -> 0; matrix products, arithmetic and copies ran while one was open for 8% -> 0% of each run, Pallas kernels for 0% -> 0%
where the time goes in v1:
time: 83.3 us; the launch traced here: 82.9 us
  Pallas kernels  77 us (92%)
  local copies, waits for them, and re-layouts  5.83 us (7%)
    pallas_call x1, Pallas kernels, body(): pl.pallas_call(functools.partial(kernel, n), out_shape=jax.ShapeDtypeStru...  77 us
    unnamed x16, local copies, waits for them, and re-layouts  5.83 us

profile of v1, /device:TPU:12, one launch (start us, length us, event | category | flops | bytes accessed | tf_op | source)
XLA Modules:
  0.0 82.9 jit_solution(7706096831685470933)
XLA Ops:
  0.0 0.0 copy-start.5
  0.0 0.8 copy.10.cross_owner
  0.8 0.0 copy-done.5
  0.8 0.1 copy.11.recoupling_index
  0.9 0.0 copy-start.3
  0.9 0.0 copy-start.4
  0.9 0.7 copy.9.cross_weights
  1.6 0.0 copy-done.3
  1.6 0.0 copy-done.4
  1.6 0.0 copy-start
  1.6 1.2 %copy-done = f32[1,1,512,512]{3,2,1,0:T(8,128)S(1)} copy-done((f32[1,1,512,512]{3,2,1,0:T(8,128)S(1)}, f32[1,1,512,512]{3,2,1,0:T(8,128)}, u32[]{:S(2)}) %copy-start) | copy-done | bytes 1048600
  2.8 0.0 copy-start.1
  2.8 1.2 %copy-done.1 = f32[1,1,512,512]{3,2,1,0:T(8,128)S(1)} copy-done((f32[1,1,512,512]{3,2,1,0:T(8,128)S(1)}, f32[1,1,512,512]{3,2,1,0:T(8,128)}, u32[]{:S(2)}) %copy-start.1) | copy-done | bytes 1048600
  4.0 0.0 copy-start.2
  4.0 0.8 %copy-done.2 = f32[8,16,16]{2,1,0:T(8,128)S(1)} copy-done((f32[8,16,16]{2,1,0:T(8,128)S(1)}, f32[8,16,16]{2,1,0:T(8,128)}, u32[]{:S(2)}) %copy-start.2) | copy-done | bytes 8216
  4.9 77.0 %shard_map.82 = f32[1,1,512,512]{3,2,1,0:T(8,128)S(1)} custom-call(f32[1,1,512,512]{3,2,1,0:T(8,128)S(1)} %copy-done, f32[1,1,512,512]{3,2,1,0:T(8,128)S(1)} %copy-done.1, f32[1,1,512]{2,1,0:T(1,128)S(1)} %copy-done.3, f32[1,1,3,512]{3,2,1,0:T(4,128)S(1)} %copy.9.cross_weights, f32[8,16,16]{2,1,0:T(8,128)S(1)} %copy-done.2, s32[4,1]{1,0:T(4,128)S(1)} %copy.10.cross_owner, ...), custom_call_target="tpu_custom_call" | custom-call | tf_op jit(solution)/shard_map/pallas_call | solution.py:319
  81.9 1.0 %copy.13 = f32[1,1,512,512]{3,2,1,0:T(8,128)} copy(f32[1,1,512,512]{3,2,1,0:T(8,128)S(1)} %shard_map.82) | data formatting | bytes 2097152
Async XLA Ops:
  0.0 0.8 copy-start.5
  0.9 0.7 copy-start.3
  0.9 0.7 copy-start.4
  1.6 1.2 %copy-start = (f32[1,1,512,512]{3,2,1,0:T(8,128)S(1)}, f32[1,1,512,512]{3,2,1,0:T(8,128)}, u32[]{:S(2)}) copy-start(f32[1,1,512,512]{3,2,1,0:T(8,128)} %generator.1) | copy-start | bytes 3145732
  2.8 1.2 %copy-start.1 = (f32[1,1,512,512]{3,2,1,0:T(8,128)S(1)}, f32[1,1,512,512]{3,2,1,0:T(8,128)}, u32[]{:S(2)}) copy-start(f32[1,1,512,512]{3,2,1,0:T(8,128)} %hamiltonian.1) | copy-start | bytes 3145732
  4.0 0.8 %copy-start.2 = (f32[8,16,16]{2,1,0:T(8,128)S(1)}, f32[8,16,16]{2,1,0:T(8,128)}, u32[]{:S(2)}) copy-start(f32[8,16,16]{2,1,0:T(8,128)} %recoupling.1) | copy-start | bytes 24580

commit v2 on v1

--- a/solution.py
+++ b/solution.py
@@ -49,15 +49,20 @@
     n,
     generator,
     hamiltonian,
+    pair_weights_far,
+    cross_weights,
+    recoupling_far,
+    cross_owner_far,
+    tile_order_far,
+    recoupling_index_far,
+    out,
+    generator_tiles,
+    hamilton_tiles,
     pair_weights,
-    cross_weights,
     recoupling,
     cross_owner,
     tile_order,
     recoupling_index,
-    out,
-    generator_tiles,
-    hamilton_tiles,
     send,
     recv,
     weights_send,
@@ -70,12 +75,15 @@
     back,
     back_turned,
     inverse,
+    result,
     send_sem,
     recv_sem,
     weights_send_sem,
     weights_recv_sem,
     back_send_sem,
     back_recv_sem,
+    tile_sem,
+    small_sem,
 ):
     me = lax.axis_index("chan")
     order = generator.shape[-1]
@@ -83,7 +91,7 @@
     tiles = tile_order.shape[-1]
     spread = tiles // n
     chunks = TS // CHUNK
-    hosted = cross_weights.shape[2]
+    hosted = cross_weights.shape[1]
 
     def partner(d):
         p, bit = me, 1
@@ -100,13 +108,34 @@
     for d in distances:
         pl.semaphore_signal(barrier, inc=1, device_id={"chan": partners[d]}, device_id_type=MESH)
 
-    for slot in range(hosted):
-        weights_send[slot] = cross_weights[0, 0, slot : slot + 1, :]
-    weights_recv[me] = weights_send[...]
+    small_pairs = (
+        (tile_order_far, tile_order),
+        (cross_owner_far, cross_owner),
+        (recoupling_index_far, recoupling_index),
+        (cross_weights.at[0], weights_send),
+        (pair_weights_far, pair_weights),
+        (recoupling_far, recoupling),
+    )
+    fetches = [
+        pltpu.make_async_copy(far, near, small_sem.at[at])
+        for at, (far, near) in enumerate(small_pairs)
+    ]
+    fetches[0].start()
     for q in range(tiles):
         here, there = pl.ds((q // blocks) * TS, TS), pl.ds((q % blocks) * TS, TS)
-        generator_tiles[q] = generator[0, 0, here, there]
-        hamilton_tiles[q] = hamiltonian[0, 0, here, there]
+        for s, (far, near) in enumerate(
+            ((generator, generator_tiles), (hamiltonian, hamilton_tiles))
+        ):
+            fetch = pltpu.make_async_copy(
+                far.at[0, 0, here, there], near.at[q], tile_sem.at[s, q]
+            )
+            fetch.start()
+            fetches.append(fetch)
+    for fetch in fetches[1 : len(small_pairs)]:
+        fetch.start()
+    for fetch in fetches:
+        fetch.wait()
+    weights_recv[me] = weights_send[...]
 
     def pack(ch, target, slot):
         for r in range(spread):
@@ -176,10 +205,15 @@
     pair_row = pair_weights[0]
 
     def split_direct(step, carry):
-        rows = pl.ds(pl.multiple_of(step * SUB, SUB), SUB)
-        every = slice(None)
-        store_factor(left, right, 0, rows, every, generator[0, 0, rows, :], pair_row)
-        store_factor(left, right, 1, rows, every, hamiltonian[0, 0, rows, :], -pair_row)
+        a, part = lax.div(step, TS // SUB), lax.rem(step, TS // SUB)
+        from_rows = pl.ds(pl.multiple_of(part * SUB, SUB), SUB)
+        to_rows = pl.ds(pl.multiple_of(step * SUB, SUB), SUB)
+        for b in range(blocks):
+            cols = slice(b * TS, (b + 1) * TS)
+            row = pair_row[:, cols]
+            x, y = generator_tiles[a * blocks + b, from_rows], hamilton_tiles[a * blocks + b, from_rows]
+            store_factor(left, right, 0, to_rows, cols, x, row)
+            store_factor(left, right, 1, to_rows, cols, y, -row)
         return carry
 
     lax.fori_loop(0, order // SUB, split_direct, 0)
@@ -198,17 +232,17 @@
 
     lax.fori_loop(0, tiles, invert, 0)
 
-    owner = cross_owner[me, 0]
+    owner = cross_owner[0, me]
     slot_at = jnp.int32(0)
     for g in range(n):
         slot_at = slot_at + jnp.where(
-            jnp.logical_and(g < me, cross_owner[g, 0] == owner), 1, 0
+            jnp.logical_and(g < me, cross_owner[0, g] == owner), 1, 0
         )
     slot_at = jnp.minimum(slot_at, hosted - 1)
     for d in distances:
         weights_copy(d, partners[d]).wait_recv()
     cross_row = weights_recv[owner, slot_at]
-    matrix = recoupling_index[me, 0]
+    matrix = recoupling_index[0, me]
 
     def mix_chunk(ch, carry):
         for d in distances:
@@ -265,13 +299,17 @@
         back_copy(d, partners[d]).wait_recv()
         turn(partners[d])
 
+    writes = []
     for q in range(tiles):
         a, b = q // blocks, q % blocks
         at, turned_at = inverse[q], inverse[b * blocks + a]
         came = back[lax.div(at, spread), lax.rem(at, spread)]
         turned = back_turned[lax.div(turned_at, spread), lax.rem(turned_at, spread)]
         here, there = pl.ds(a * TS, TS), pl.ds(b * TS, TS)
-        out[0, 0, here, there] = direct[here, there] + 0.5 * (came + turned)
+        result[q] = direct[here, there] + 0.5 * (came + turned)
+        write = pltpu.make_async_copy(result.at[q], out.at[0, 0, here, there], tile_sem.at[0, q])
+        write.start()
+        writes.append(write)
 
     for d in distances:
         weights_copy(d, me).wait_send()
@@ -283,6 +321,8 @@
         return carry
 
     lax.fori_loop(0, chunks, finish, 0)
+    for write in writes:
+        write.wait()
 
 
 def solution(mesh):
@@ -314,16 +354,19 @@
         chunks = TS // CHUNK
         hosted = cross_weights.shape[2]
         f32, bf16 = jnp.float32, jnp.bfloat16
-        vmem = pl.BlockSpec(memory_space=pltpu.VMEM)
-        smem = pl.BlockSpec(memory_space=pltpu.SMEM)
         return pl.pallas_call(
             functools.partial(kernel, n),
             out_shape=jax.ShapeDtypeStruct(generator.shape, f32),
-            in_specs=[vmem] * 4 + [smem] * 4,
-            out_specs=vmem,
+            in_specs=[pl.BlockSpec(memory_space=pltpu.HBM)] * 8,
+            out_specs=pl.BlockSpec(memory_space=pltpu.HBM),
             scratch_shapes=[
                 pltpu.VMEM((tiles, TS, TS), f32),
                 pltpu.VMEM((tiles, TS, TS), f32),
+                pltpu.VMEM(pair_weights.shape, f32),
+                pltpu.SMEM(recoupling.shape, f32),
+                pltpu.SMEM((1, n), jnp.int32),
+                pltpu.SMEM(tile_order.shape, jnp.int32),
+                pltpu.SMEM((1, n), jnp.int32),
                 pltpu.VMEM((chunks, n, 2, spread, CHUNK, TS), f32),
                 pltpu.VMEM((chunks, n, 2, spread, CHUNK, TS), f32),
                 pltpu.VMEM((hosted, 1, order), f32),
@@ -336,25 +379,28 @@
                 pltpu.VMEM((n, spread, TS, TS), f32),
                 pltpu.VMEM((n, spread, TS, TS), f32),
                 pltpu.SMEM((tiles,), jnp.int32),
+                pltpu.VMEM((tiles, TS, TS), f32),
                 pltpu.SemaphoreType.DMA((chunks, n)),
                 pltpu.SemaphoreType.DMA((chunks, n)),
                 pltpu.SemaphoreType.DMA((n,)),
                 pltpu.SemaphoreType.DMA((n,)),
                 pltpu.SemaphoreType.DMA((n,)),
                 pltpu.SemaphoreType.DMA((n,)),
+                pltpu.SemaphoreType.DMA((2, tiles)),
+                pltpu.SemaphoreType.DMA((6,)),
             ],
             compiler_params=pltpu.CompilerParams(
-                collective_id=0, has_side_effects=True, vmem_limit_bytes=48 * 1024 * 1024
+                collective_id=0, has_side_effects=True, vmem_limit_bytes=64 * 1024 * 1024
             ),
         )(
             generator,
             hamiltonian,
             pair_weights,
-            cross_weights,
+            jnp.swapaxes(cross_weights, 1, 2),
             recoupling,
-            cross_owner,
+            jnp.transpose(cross_owner),
             tile_order,
-            recoupling_index,
+            jnp.transpose(recoupling_index),
         )
 
     return jax.shard_map(

time: 83.3 us -> 79.1 us (0.950)
  local copies, waits for them, and re-layouts: 5.83 us -> 2.26 us
    unnamed x16 -> x1, local copies, waits for them, and re-layouts: 5.83 us -> 2.26 us
where the time goes in v2:
time: 79.1 us; the launch traced here: 78.7 us
  Pallas kernels  76.4 us (97%)
  local copies, waits for them, and re-layouts  2.26 us (3%)
    pallas_call x1, Pallas kernels, body(): pl.pallas_call(functools.partial(kernel, n), out_shape=jax.ShapeDtypeStru...  76.4 us
    unnamed x1, local copies, waits for them, and re-layouts  2.26 us

profile of v2, /device:TPU:12, one launch (start us, length us, event | category | flops | bytes accessed | tf_op | source)
XLA Modules:
  0.0 78.7 jit_solution(13670615321491375200)
XLA Ops:
  0.0 76.4 %shard_map.82 = f32[1,1,512,512]{3,2,1,0:T(8,128)} custom-call(f32[1,1,512,512]{3,2,1,0:T(8,128)} %generator.1, f32[1,1,512,512]{3,2,1,0:T(8,128)} %hamiltonian.1, f32[1,1,512]{2,1,0:T(1,128)} %pair_weights_far.1, f32[1,3,1,512]{3,2,1,0:T(1,128)} %bitcast.3, f32[8,16,16]{2,1,0:T(8,128)} %recoupling_far.1, s32[1,4]{1,0:T(1,128)} %bitcast.4, ...), custom_call_target="tpu_custom_call" | custom-call | tf_op jit(solution)/shard_map/pallas_call | solution.py:357
  76.4 2.3 %copy.10 = f32[1,1,512,512]{3,2,1,0:T(8,128)} copy(f32[1,1,512,512]{3,2,1,0:T(8,128)} %shard_map.82) | data formatting | bytes 2097152
